TPU v7x, 32 devices: a whole 2x2x4 slice. The times are simulated.
32 devices in a mesh: beam: 4 (over y, x), ma: 8 (over z, core).
Axes of the slice: x: 2, y: 2, z: 4, core: 2. Of those that a mesh axis runs over, the one named last changes fastest.
Arguments:
- sky_harmonics: float32 [16, 2, 2048], P('ma'), may hold values from -6 to 6
- beam_harmonics: float32 [32, 2, 2048], P('beam'), may hold values from -6 to 6
- wigner: bfloat16 [32, 16, 16, 2048], P('beam', 'ma'), may hold values from -0.125 to 0.125
- order_map: int32 [16], replicated, may hold values from 0 to 2047, as said below
- block_owner: int32 [1024, 1], P('ma'), may hold values from 0 to 7; in each aligned block of 128 rows (0 to 127, 128 to 255, ...) at most 32 rows name the same one
- block_local: int32 [1024], P('ma'), may hold values from 0 to 63
- cell_offset: int32 [131072], P('ma'), may hold values from 0 to 126
- cell_fraction: float32 [131072], P('ma'), may hold values from 0 to 1
- beam_angle: float32 [131072], P('ma'), may hold values from -3.140625 to 3.140625
- sample_count: int32 [8], P('ma'), may hold values from 1 to 16384, 98304 in all
- noise_weight: float32 [128, 128], replicated, may hold values from -0.2 to 2, as said below
Outputs:
- sky_gradient: float32 [16, 2, 2048], P('ma', None, 'beam')
Inputs may be any that keep to these rules, and one draw needn't show every extreme that they name: `order_map`: 16 distinct azimuthal orders. `block_owner`: among the 128 sample blocks of one device, at most 32 name the same owner, and in some device some owner is named exactly 32 times. `noise_weight`: diagonal entries lie in 1 to 2, the others within 0.2 in magnitude.
All inputs are finite; a program needn't handle non-finite values. No bound on the sum of `sample_count` on one device may be relied on, other than what follows from the above.
Results may differ from a plain program's by a relative error of at most 0.017.
Values may be sent and summed in bfloat16 or wider, within the bound.
No kernel may reach another device: no remote copies, remote signals or barrier semaphores. Data moves between devices by JAX's collectives and lax.ppermute only.
A program may use at most 128 MiB of HBM per device.

v0:
```python
import functools
import math

import jax
import jax.numpy as jnp
from jax import lax
from jax.experimental import pallas as pl
from jax.experimental.pallas import tpu as pltpu
from jax.sharding import PartitionSpec as P

PHI = 4096
CELLS = 128
CYCLE_BLOCKS = PHI // CELLS
F32 = jnp.float32
BF16 = jnp.bfloat16
LAST_LAST = (((1,), (1,)), ((), ()))


def iota(shape, axis):
    return lax.broadcasted_iota(jnp.int32, shape, axis)


def vmem(count):
    return [pl.BlockSpec(memory_space=pltpu.VMEM)] * count


def smem(count):
    return [pl.BlockSpec(memory_space=pltpu.SMEM)] * count


def hbm(count):
    return [pl.BlockSpec(memory_space=pltpu.HBM)] * count


def sine_turns(z):
    square = z * z
    value = 39.53670603 * square - 76.54978229
    value = value * square + 81.60100407
    value = value * square - 41.34165503
    value = value * square + 6.28318516
    return value * z


def cosine_steps(steps):
    centred = ((steps + PHI // 2) & (PHI - 1)) - PHI // 2
    return sine_turns(0.25 - jnp.abs(centred).astype(F32) * (1.0 / PHI))


def every(ref, first, count, step):
    if ref.shape[1] == CELLS:
        return ref[pl.ds(first, count, stride=step), :]
    return jnp.concatenate([ref[first + i * step][None] for i in range(count)], axis=0)


def put_every(ref, first, step, values):
    if ref.shape[1] == CELLS:
        ref[pl.ds(first, values.shape[0], stride=step), :] = values
    else:
        for i in range(values.shape[0]):
            ref[first + i * step, :] = values[i]


def bring(sources, places, semaphores, first):
    copies = [
        pltpu.make_async_copy(source, place, semaphores.at[first + i])
        for i, (source, place) in enumerate(zip(sources, places))
    ]
    for copy in copies:
        copy.start()
    return copies


def own_block(orders, cycles):
    shape = (orders, orders * cycles)
    return iota(shape, 1) // cycles == iota(shape, 0)


def modes_kernel(sky_hbm, beam_hbm, wigner_hbm, later_hbm, out, later, sky, beam, wigner, arrivals):
    chunks, orders, sky_orders, cycles, width = wigner.shape
    small = bring((sky_hbm, beam_hbm), (sky, beam), arrivals, 0)
    spans = [pl.ds(i * width, width) for i in range(chunks)]
    large = bring([wigner_hbm.at[:, :, :, span] for span in spans], [wigner.at[i] for i in range(chunks)], arrivals, 2)
    places = [
        place if place.shape == source.shape else place.at[0 : source.shape[0]]
        for source, place in zip(later_hbm, later)
    ]
    others = bring(later_hbm, places, arrivals, 2 + chunks)
    for copy in small:
        copy.wait()
    beam_real, beam_imag = beam[:, 0, :], beam[:, 1, :]
    diagonal = own_block(orders, cycles)
    products = []
    for m in range(sky_orders):
        sky_real, sky_imag = sky[m, 0:1, :], sky[m, 1:2, :]
        first = sky_real * beam_real - sky_imag * beam_imag
        second = sky_real * beam_imag + sky_imag * beam_real
        products.append(jnp.concatenate([first, second], axis=0).astype(BF16))
    sums = [0.0] * sky_orders
    for i in range(chunks):
        large[i].wait()
        for m in range(sky_orders):
            table = wigner[i, :, m].reshape(orders * cycles, width)
            left = products[m][:, i * width : (i + 1) * width]
            sums[m] += lax.dot_general(table, left, LAST_LAST, preferred_element_type=F32)
    rows = [None] * (2 * sky_orders)
    for m in range(sky_orders):
        modes = sums[m].T
        for c in range(2):
            part = jnp.where(diagonal, modes[c * orders : (c + 1) * orders], 0.0)
            rows[c * sky_orders + m] = jnp.sum(part, axis=0, keepdims=True)
    block = jnp.concatenate(rows + rows, axis=0).astype(BF16)
    for d in range(out.shape[0]):
        out[d] = block
    for copy in others:
        copy.wait()


def tables_kernel(
    blocks_local, sky_devices,
    order_vmem, owners_vmem, locals_vmem, angles, offsets, fractions, beam_hbm, wigner_hbm,
    phi, turn, own, pieces_hbm, pieces, beam, departures, order_map, owners, locals_, arrivals,
    step_real, step_imag, powers,
):
    copies = bring((order_vmem, owners_vmem, locals_vmem), (order_map, owners, locals_), arrivals, 0)
    me = lax.axis_index("beam")
    extra = bring((beam_hbm,), (beam,), arrivals, 3)[0]
    beams, beam_orders, width = pieces.shape[0], beam.shape[0], pieces.shape[4]
    spans = [pl.ds(pl.multiple_of((me ^ j) * width, width), width) for j in range(beams)]
    arriving = [
        pltpu.make_async_copy(wigner_hbm.at[:, :, :, span], pieces.at[j, 0:beam_orders], departures.at[j])
        for j, span in enumerate(spans)
    ]
    for j in [*range(1, beams), 0]:
        arriving[j].start()
    orders = order_map.shape[0]
    blocks = angles.shape[0]
    half = turn.shape[0] // blocks // 2
    own_half = own.shape[0] // blocks // 2

    part = angles[...] * (0.5 / math.pi)
    part = part - jnp.round(part)
    folded = jnp.where(part > 0.25, 0.5 - part, jnp.where(part < -0.25, -0.5 - part, part))
    real, imag = sine_turns(0.25 - jnp.abs(part)), sine_turns(folded)
    for i in range(4):
        if i:
            real, imag = real * real - imag * imag, 2.0 * real * imag
        powers[2 * i, 0:blocks], powers[2 * i + 1, 0:blocks] = real, imag

    copies[0].wait()
    order = jnp.zeros((orders, CELLS), jnp.int32)
    row = iota((orders, CELLS), 0)
    lane = iota((orders, CELLS), 1)
    for m in range(orders):
        place = m % (orders // sky_devices) * sky_devices + m // (orders // sky_devices)
        order = jnp.where(row == place, order_map[m], order)

    def phase(steps):
        return cosine_steps(steps), cosine_steps(steps + PHI // 4)

    scaling = 1.0 / math.sqrt(orders)
    cell_real, cell_imag = phase(order * lane)
    cell_real, cell_imag = cell_real * scaling, cell_imag * scaling
    next_real, next_imag = phase(order)
    next_real = next_real - 1.0
    first_real, first_imag = phase(((order * CELLS) & (PHI - 1)) * lane)
    for j in range(CYCLE_BLOCKS):
        step_real[j] = jnp.broadcast_to(first_real[:, j : j + 1], (orders, CELLS))
        step_imag[j] = jnp.broadcast_to(first_imag[:, j : j + 1], (orders, CELLS))
    for copy in copies[1:]:
        copy.wait()

    def block_phases(s):
        place = (owners[s] * blocks_local + locals_[s]) & (CYCLE_BLOCKS - 1)
        offset = offsets[pl.ds(s, orders, stride=0), :]
        fraction = fractions[pl.ds(s, orders, stride=0), :]
        real = jnp.take_along_axis(cell_real, offset, axis=1, mode="promise_in_bounds")
        imag = jnp.take_along_axis(cell_imag, offset, axis=1, mode="promise_in_bounds")
        base_real, base_imag = step_real[place], step_imag[place]
        left_real = real * base_real - imag * base_imag
        left_imag = real * base_imag + imag * base_real
        mix_real = 1.0 + fraction * next_real
        mix_imag = fraction * next_imag
        both = jnp.concatenate(
            [left_real * mix_real - left_imag * mix_imag, left_real * mix_imag + left_imag * mix_real],
            axis=0,
        )
        start = pl.multiple_of(s * 2 * orders, 2 * orders)
        phi[pl.ds(start, 2 * orders), :] = both.astype(BF16)

    scale = 1.0 / math.sqrt(2 * half)
    power = iota((8, CELLS), 0)

    def block_turns(s):
        steps = [powers[i, pl.ds(s, 8, stride=0), :] for i in range(8)]
        one_real, one_imag = steps[:2]
        step = steps[6:]
        odd = power & 1 == 1
        real, imag = jnp.where(odd, one_real * scale, scale), jnp.where(odd, one_imag * scale, 0.0)
        for bit in (2, 4):
            taken = power & bit == bit
            by_real, by_imag = jnp.where(taken, steps[bit], 1.0), jnp.where(taken, steps[bit + 1], 0.0)
            real, imag = real * by_real - imag * by_imag, real * by_imag + imag * by_real
        evens, odds = [], []
        for j in range(half // 8):
            if j:
                real, imag = real * step[0] - imag * step[1], real * step[1] + imag * step[0]
            evens.append(real)
            odds.append(real * one_imag + imag * one_real)
        return evens + odds

    some = max(2, CELLS // (2 * half))
    shape = (some * 2 * own_half, some * 2 * half)
    own_row, turn_row = iota(shape, 0), iota(shape, 1)
    kept = own_row % (2 * own_half)
    source = kept // own_half * half + me * own_half + kept % own_half
    chosen = turn_row == own_row // (2 * own_half) * (2 * half) + source
    chosen = jnp.where(chosen, 1.0, 0.0).astype(BF16)
    run = 32

    def one_run(group):
        for j in range(0, run, some):
            first = group * run + j
            rows = []
            for i in range(some):
                block_phases(first + i)
                rows += block_turns(first + i)
            rows = jnp.concatenate(rows, axis=0).astype(BF16)
            turn[pl.ds(pl.multiple_of(first * 2 * half, shape[1]), shape[1]), :] = rows
            mine = jnp.dot(chosen, rows, preferred_element_type=F32)
            own[pl.ds(pl.multiple_of(first * 2 * own_half, shape[0]), shape[0]), :] = mine.astype(BF16)

    def beam_terms():
        extra.wait()
        sky_orders, cycles = pieces.shape[2:4]
        for j, span in enumerate(spans):
            terms = []
            for c in range(2):
                values = beam[:, c, span]
                high = values.astype(BF16)
                terms += [high, (values - high.astype(F32)).astype(BF16)]
            filling = sky_orders * cycles - 4 * beam_orders
            if filling:
                terms.append(jnp.zeros((filling, width), BF16))
            pieces[j, beam_orders] = jnp.concatenate(terms, axis=0).reshape(sky_orders, cycles, width)

    runs = blocks // run
    turns = [*range(1, beams), 0]

    def leaving(j):
        return pltpu.make_async_copy(pieces.at[j], pieces_hbm[j], departures.at[beams + j])

    @pl.loop(0, runs)
    def _(group):
        one_run(group)
        pl.when(group == 0)(beam_terms)
        for i, j in enumerate(turns):

            @pl.when(group == i * (runs // 2) // beams)
            def _(j=j):
                arriving[j].wait()
                leaving(j).start()

    for j in range(beams):
        leaving(j).wait()


def samples_kernel(
    blocks_local, rows, owners_vmem, locals_vmem, count, noise, arrived, phi, turn, own,
    out, owners, locals_, arrivals, widened,
    stacked, modes_rows, modes, partial, filtered, totals, ordered, shares,
):
    copies = bring((owners_vmem, locals_vmem), (owners, locals_), arrivals, 0)
    widened[...] = arrived[...].astype(F32)
    lanes = shares.shape[1]
    parts = shares.shape[0]
    beams = arrived.shape[0] // parts
    sky_devices = parts // rows
    blocks = partial.shape[0] // 8
    total = turn.shape[0] // blocks
    orders = total // beams
    cycles = lanes // orders
    together = len(totals)
    unroll = 32

    steps = max(1, blocks // (together * unroll))

    def cycle_of(s):
        return (owners[s] * blocks_local + locals_[s]) // CYCLE_BLOCKS

    width = together * parts
    for b in range(beams):
        for row in range(rows):
            some = every(widened, b * parts + row, sky_devices, rows)
            for j in range(together):
                start = j * parts + row * sky_devices
                stacked[b, start : start + sky_devices, :] = some
        modes_rows[b * lanes : (b + 1) * lanes, :] = stacked[b].T
    lane_group = iota((total, width), 1) // parts
    for r in range(cycles):
        halves = [
            modes_rows[pl.ds(r + parity * cycles, total // 2, stride=2 * cycles), :]
            for parity in range(2)
        ]
        values = jnp.concatenate(halves, axis=0)
        for j in range(together):
            modes[r, j] = jnp.where(lane_group == j, values, 0.0).astype(BF16)
    for copy in copies:
        copy.wait()

    def gather(first):
        left = jnp.concatenate([modes[cycle_of(first + j), j] for j in range(together)], axis=0)
        table = phi[pl.ds(pl.multiple_of(first * parts, width), width), :]
        cells = jnp.dot(left, table, preferred_element_type=F32)
        rotation = turn[pl.ds(pl.multiple_of(first * total, together * total), together * total), :]
        turned = (cells * rotation.astype(F32)).reshape(together, total // 8, 8, CELLS)
        kept = jnp.sum(turned, axis=1).reshape(together * 8, CELLS)
        partial[pl.ds(pl.multiple_of(first * 8, together * 8), together * 8), :] = kept

    @pl.loop(0, steps)
    def _(step):
        for i in range(unroll):
            gather((step * unroll + i) * together)

    signal = partial[pl.ds(0, blocks, stride=8), :]
    for i in range(1, 8):
        signal = signal + partial[pl.ds(i, blocks, stride=8), :]
    valid = iota((blocks, CELLS), 0) * CELLS + iota((blocks, CELLS), 1) < count[0:1, :]
    signal = jnp.where(valid, signal, 0.0)
    clean = lax.dot_general(
        signal.astype(BF16), noise[...].astype(BF16), LAST_LAST, preferred_element_type=F32
    )
    filtered[0:blocks] = jnp.where(valid, clean, 0.0)

    for one in totals:
        one[...] = jnp.zeros_like(one)
    half = orders // 2

    def spread(first):
        rotation = own[pl.ds(pl.multiple_of(first * orders, 16), together * orders), :].astype(F32)
        weighted = [
            rotation[j * orders : (j + 1) * orders] * filtered[pl.ds(first + j, orders, stride=0), :]
            for j in range(together)
        ]
        weighted = jnp.concatenate(weighted, axis=0).astype(BF16)
        table = phi[pl.ds(pl.multiple_of(first * parts, width), width), :]
        terms = lax.dot_general(weighted, table, LAST_LAST, preferred_element_type=F32)
        for j in range(together):
            row = pl.multiple_of(cycle_of(first + j) * orders, orders)
            here = totals[j]
            here[pl.ds(row, orders), :] += terms[j * orders : (j + 1) * orders]

    @pl.loop(0, steps)
    def _(step):
        for i in range(unroll):
            spread((step * unroll + i) * together)

    gathered = totals[0][...]
    which = iota(gathered.shape, 1) // parts
    for j in range(1, together):
        gathered = jnp.where(which == j, totals[j][...], gathered)
    totals[0][...] = gathered
    for k in range(orders):
        place = k // 2 + (k % 2) * half
        ordered[k * cycles : (k + 1) * cycles, :] = totals[0][pl.ds(place, cycles, stride=orders), :]
    turned = ordered[...].T
    summed = turned[0:parts]
    for j in range(1, together):
        summed = summed + turned[j * parts : (j + 1) * parts]
    for row in range(rows):
        put_every(shares, row, rows, summed[row * sky_devices : (row + 1) * sky_devices])
    block = shares[...].astype(BF16)
    for b in range(beams):
        out[b] = block


def gradient_kernel(arrived, pieces, out, modes):
    me = lax.axis_index("beam")
    parts, sky_orders, cycles, width = pieces[0].shape
    orders = parts - 1
    diagonal = own_block(orders, cycles)
    for b in range(len(pieces)):
        terms = arrived[b].astype(F32)
        while terms.shape[0] > 2 * sky_orders:
            middle = terms.shape[0] // 2
            terms = terms[:middle] + terms[middle:]
        modes[b] = terms.astype(BF16).astype(F32)
    first, second = [0.0] * sky_orders, [0.0] * sky_orders
    for j, piece in enumerate(pieces):
        terms = piece[orders].reshape(sky_orders * cycles, width).astype(F32)
        beam_real, beam_imag = [
            terms[2 * c * orders : (2 * c + 1) * orders] + terms[(2 * c + 1) * orders : (2 * c + 2) * orders]
            for c in range(2)
        ]
        these = modes[me ^ j]
        for m in range(sky_orders):
            spreads = []
            for c in range(2):
                row = these[c * sky_orders + m : c * sky_orders + m + 1]
                spreads.append(jnp.where(diagonal, row, 0.0))
            left = jnp.concatenate(spreads, axis=0).astype(BF16)
            table = piece[0:orders, m].reshape(orders * cycles, width)
            harmonics = jnp.dot(left, table, preferred_element_type=F32)
            real, imag = harmonics[:orders], harmonics[orders:]
            first[m] += real * beam_real + imag * beam_imag
            second[m] += imag * beam_real - real * beam_imag
    for m in range(sky_orders):
        out[m, 0:1, :] = jnp.sum(first[m], axis=0, keepdims=True)
        out[m, 1:2, :] = jnp.sum(second[m], axis=0, keepdims=True)


def exchange(pieces, axis):
    count = lax.axis_size(axis)
    moved = {j: lax.ppermute(pieces[j], axis, [(i, i ^ j) for i in range(count)]) for j in range(count - 1, 0, -1)}
    return [pieces[0]] + [moved[j] for j in range(1, count)]


def local(
    sky_harmonics,
    beam_harmonics,
    wigner,
    order_map,
    block_owner,
    block_local,
    cell_offset,
    cell_fraction,
    beam_angle,
    sample_count,
    noise_weight,
):
    beams, sky_devices = lax.axis_size("beam"), lax.axis_size("ma")
    orders, sky_orders, cycles, degrees = wigner.shape
    total = orders * beams
    all_sky = sky_orders * sky_devices
    parts = 2 * all_sky
    blocks = block_local.shape[0]
    blocks_local = cycles // sky_devices * CYCLE_BLOCKS
    width = degrees // beams
    lanes = orders * cycles
    rows = 2 * sky_orders
    together = max(1, CELLS // parts)
    owners = block_owner.reshape(blocks)
    limit = pltpu.CompilerParams(vmem_limit_bytes=32 * 1024 * 1024)
    integers = [
        pltpu.SMEM((blocks,), jnp.int32),
        pltpu.SMEM((blocks,), jnp.int32),
    ]

    def pinned(*arrays):
        return [pltpu.with_memory_space_constraint(array, pltpu.HBM) for array in arrays]

    later = (
        order_map, owners, block_local,
        beam_angle.reshape(blocks, CELLS),
        cell_offset.reshape(blocks, CELLS),
        cell_fraction.reshape(blocks, CELLS),
        noise_weight,
    )
    sent, (order_map, owners, places, angles, offsets, fractions, noise) = pl.pallas_call(
        modes_kernel,
        out_shape=[
            jax.ShapeDtypeStruct((beams * sky_devices // 2, 2 * rows, lanes), BF16),
            [
                pltpu.VMEM((blocks + all_sky, CELLS) if place in (4, 5) else array.shape, array.dtype)
                for place, array in enumerate(later)
            ],
        ],
        in_specs=[*hbm(3), hbm(len(later))],
        out_specs=[vmem(1)[0], vmem(len(later))],
        scratch_shapes=[
            pltpu.VMEM(sky_harmonics.shape, F32),
            pltpu.VMEM(beam_harmonics.shape, F32),
            pltpu.VMEM((beams, orders, sky_orders, cycles, width), BF16),
            pltpu.SemaphoreType.DMA((2 + beams + len(later),)),
        ],
        compiler_params=limit,
        name="modes",
    )(*pinned(sky_harmonics, beam_harmonics, wigner), pinned(*later))
    sent = sent.reshape(beams * sky_devices, rows, lanes)
    arrived = lax.all_to_all(sent, ("beam", "ma"), split_axis=0, concat_axis=0, tiled=True)

    samples = pltpu.VMEM((blocks, CELLS), F32)
    piece = (orders + 1, sky_orders, cycles, width)
    phi, turn, own, pieces = pl.pallas_call(
        functools.partial(tables_kernel, blocks_local, sky_devices),
        out_shape=[
            pltpu.VMEM((blocks * parts, CELLS), BF16),
            pltpu.VMEM((blocks * total, CELLS), BF16),
            pltpu.VMEM((blocks * orders, CELLS), BF16),
            [pltpu.HBM(piece, BF16)] * beams,
        ],
        in_specs=vmem(6) + hbm(2),
        out_specs=[*vmem(3), hbm(beams)],
        scratch_shapes=[
            pltpu.VMEM((beams, *piece), BF16),
            pltpu.VMEM(beam_harmonics.shape, F32),
            pltpu.SemaphoreType.DMA((2 * beams,)),
            pltpu.SMEM((all_sky,), jnp.int32),
            *integers,
            pltpu.SemaphoreType.DMA((4,)),
            pltpu.VMEM((CYCLE_BLOCKS, all_sky, CELLS), F32),
            pltpu.VMEM((CYCLE_BLOCKS, all_sky, CELLS), F32),
            pltpu.VMEM((8, blocks + 8, CELLS), F32),
        ],
        compiler_params=limit,
        cost_estimate=pl.CostEstimate(flops=100_000_000, bytes_accessed=4_000_000, transcendentals=0),
        name="tables",
    )(
        order_map, owners, places, angles, offsets, fractions,
        *pinned(beam_harmonics, wigner),
    )
    pieces = exchange(pieces, "beam")

    grads = pl.pallas_call(
        functools.partial(samples_kernel, blocks_local, rows),
        out_shape=jax.ShapeDtypeStruct((beams, parts, lanes), BF16),
        in_specs=vmem(8),
        out_specs=vmem(1)[0],
        scratch_shapes=[
            *integers,
            pltpu.SemaphoreType.DMA((2,)),
            pltpu.VMEM((beams * parts, lanes), F32),
            pltpu.VMEM((beams, together * parts, lanes), F32),
            pltpu.VMEM((beams * lanes, together * parts), F32),
            pltpu.VMEM((cycles, together, total, together * parts), BF16),
            pltpu.VMEM((blocks * 8, CELLS), F32),
            pltpu.VMEM((blocks + orders, CELLS), F32),
            [pltpu.VMEM((lanes, together * parts), F32) for _ in range(together)],
            pltpu.VMEM((lanes, together * parts), F32),
            pltpu.VMEM((parts, lanes), F32),
        ],
        compiler_params=limit,
        cost_estimate=pl.CostEstimate(flops=40_000_000_000, bytes_accessed=100_000_000, transcendentals=0),
        name="samples",
    )(
        owners, places, jnp.broadcast_to(sample_count[None, :], (8, CELLS)), noise,
        arrived.reshape(beams * parts, lanes), phi, turn, own,
    )
    grads = grads.reshape(beams * sky_devices, rows, lanes)
    grads = lax.all_to_all(grads, ("beam", "ma"), split_axis=0, concat_axis=0, tiled=True)
    return pl.pallas_call(
        gradient_kernel,
        out_shape=jax.ShapeDtypeStruct((sky_orders, 2, width), F32),
        in_specs=[vmem(1)[0], vmem(beams)],
        out_specs=vmem(1)[0],
        scratch_shapes=[pltpu.VMEM((beams, rows, lanes), F32)],
        compiler_params=limit,
        name="gradient",
    )(grads.reshape(beams, parts, lanes), pieces)


def solution(mesh):
    return jax.shard_map(
        local,
        mesh=mesh,
        in_specs=(
            P("ma", None, None),
            P("beam", None, None),
            P("beam", "ma", None, None),
            P(),
            P("ma", None),
            P("ma"),
            P("ma"),
            P("ma"),
            P("ma"),
            P("ma"),
            P(),
        ),
        out_specs=P("ma", None, "beam"),
        check_vma=False,
    )
```

profile of v0, /device:TPU:0, one launch (start us, length us, event | category | flops | bytes accessed | tf_op | source)
XLA Modules:
  0.0 33.1 jit_solution(6500891229384819020)
XLA Ops:
  0.0 2.3 %modes.1 = (bf16[16,8,128]{2,1,0:T(8,128)(2,1)}, s32[16]{0:T(128)S(1)}, s32[128]{0:T(128)S(1)}, s32[128]{0:T(128)S(1)}, f32[128,128]{1,0:T(8,128)S(1)}, /*index=...) custom-call(f32[2,2,2048]{2,1,0:T(2,128)} %sky_hbm.1, f32[8,2,2048]{2,1,0:T(2,128)} %beam_hbm.3, ...), custom_call_target="tpu_custom_call" | custom-call | tf_op jit(solution)/shard_map/modes/pallas_call | solution.py:458
  2.3 7.3 %all-to-all-start = ((bf16[32,4,128]{2,1,0:T(4,128)(2,1)}), bf16[32,4,128]{2,1,0:T(4,128)(2,1)S(1)}, u32[]{:S(2)}, u32[]{:S(2)}) async-start(bf16[32,4,128]{2,1,0:T(4,128)(2,1)} %bitcast.5), calls=%async_computation | async-start | bytes 65536 | tf_op jit(solution)/shard_map/all_to_all | solution.py:479
  9.6 3.1 %tables.1 = (bf16[4096,128]{1,0:T(8,128)(2,1)S(1)}, bf16[4096,128]{1,0:T(8,128)(2,1)S(1)}, bf16[1024,128]{1,0:T(8,128)(2,1)S(1)}, bf16[9,2,16,512]{3,2,1,0:T(8,1...) custom-call(s32[16]{0:T(128)S(1)} %get-tuple-element.24.order_vmem, ...), custom_call_target="tpu_custom_call" | custom-call | flops 100000000 | bytes 4000000 | tf_op jit(solution)/shard_map/tables/pallas_call | solution.py:483
  12.7 1.8 %collective-permute-start = (bf16[9,2,16,512]{3,2,1,0:T(8,128)(2,1)}, bf16[9,2,16,512]{3,2,1,0:T(8,128)(2,1)S(1)}, u32[]{:S(2)}, u32[]{:S(2)}) collective-permute-start(bf16[9,2,16,512]{3,2,1,0:T(8,128)(2,1)} %get-tuple-element.32), channel_id=1, source_target_pairs={{0,8},{8,0},{16,24},{24,16},{1,9},{9,1},{17,25},{25,17},{2,10},{10... | collective-permute-start | bytes 884744 | tf_op jit(solution)/shard_map/ppermute | solution.py:413
  14.5 1.5 %collective-permute-start.1 = (bf16[9,2,16,512]{3,2,1,0:T(8,128)(2,1)}, bf16[9,2,16,512]{3,2,1,0:T(8,128)(2,1)S(1)}, u32[]{:S(2)}, u32[]{:S(2)}) collective-permute-start(bf16[9,2,16,512]{3,2,1,0:T(8,128)(2,1)} %get-tuple-element.33), channel_id=1, source_target_pairs={{0,16},{8,24},{16,0},{24,8},{1,17},{9,25},{17,1},{25,9},{2,18},{10... | collective-permute-start | bytes 884744 | tf_op jit(solution)/shard_map/ppermute | solution.py:413
  16.0 0.3 collective-permute-start.2
  16.9 0.0 all-to-all-done
  16.9 0.0 copy-start
  16.9 2.4 %samples.1 = bf16[4,32,128]{2,1,0:T(8,128)(2,1)S(1)} custom-call(s32[128]{0:T(128)S(1)} %get-tuple-element.20.owners_vmem, s32[128]{0:T(128)S(1)} %get-tuple-element.21.locals_vmem, s32[8,128]{1,0:T(8,128)S(1)} %broadcast_in_dim.9.count, f32[128,128]{1,0:T(8,128)S(1)} %get-tuple-element.22.noise, bf16[128,128]{1,0:T(8,128)(2,1)S(1)} %bitcast.11, ...), custom_call_target="tpu_custom_call" | custom-call | flops 40000000000 | bytes 100000000 | tf_op jit(solution)/shard_map/samples/pallas_call | solution.py:513
  19.3 12.9 %all_to_all.10 = bf16[32,4,128]{2,1,0:T(4,128)(2,1)S(1)} all-to-all(bf16[32,4,128]{2,1,0:T(4,128)(2,1)S(1)} %bitcast.12), channel_id=1, replica_groups=mesh['beam'=4,'ma'=8] {'beam','ma'}, dimensions={0} | all-to-all | bytes 65536 | tf_op jit(solution)/shard_map/all_to_all | solution.py:539
  32.2 0.0 collective-permute-done.pieces_1_
  32.2 0.0 collective-permute-done.1.pieces_2_
  32.2 0.0 collective-permute-done.2.pieces_3_
  32.2 0.0 copy-done
  32.2 0.9 %gradient.1 = f32[2,2,512]{2,1,0:T(2,128)} custom-call(bf16[4,32,128]{2,1,0:T(8,128)(2,1)S(1)} %bitcast.10, bf16[9,2,16,512]{3,2,1,0:T(8,128)(2,1)S(1)} %copy-done, bf16[9,2,16,512]{3,2,1,0:T(8,128)(2,1)S(1)} %collective-permute-done.pieces_1_, bf16[9,2,16,512]{3,2,1,0:T(8,128)(2,1)S(1)} %collective-permute-done.1.pieces_2_, ...), custom_call_target="tpu_custom_call" | custom-call | tf_op jit(solution)/shard_map/gradient/pallas_call | solution.py:540
  (1 shorter events, 0.0 us)
Async XLA Ops:
  2.3 14.6 %all-to-all-start = ((bf16[32,4,128]{2,1,0:T(4,128)(2,1)}), bf16[32,4,128]{2,1,0:T(4,128)(2,1)S(1)}, u32[]{:S(2)}, u32[]{:S(2)}) async-start(bf16[32,4,128]{2,1,0:T(4,128)(2,1)} %bitcast.5), calls=%async_computation | async-start | bytes 65536 | tf_op jit(solution)/shard_map/all_to_all | solution.py:479
  12.7 19.5 %collective-permute-start = (bf16[9,2,16,512]{3,2,1,0:T(8,128)(2,1)}, bf16[9,2,16,512]{3,2,1,0:T(8,128)(2,1)S(1)}, u32[]{:S(2)}, u32[]{:S(2)}) collective-permute-start(bf16[9,2,16,512]{3,2,1,0:T(8,128)(2,1)} %get-tuple-element.32), channel_id=1, source_target_pairs={{0,8},{8,0},{16,24},{24,16},{1,9},{9,1},{17,25},{25,17},{2,10},{10... | collective-permute-start | bytes 884744 | tf_op jit(solution)/shard_map/ppermute | solution.py:413
  14.5 17.7 %collective-permute-start.1 = (bf16[9,2,16,512]{3,2,1,0:T(8,128)(2,1)}, bf16[9,2,16,512]{3,2,1,0:T(8,128)(2,1)S(1)}, u32[]{:S(2)}, u32[]{:S(2)}) collective-permute-start(bf16[9,2,16,512]{3,2,1,0:T(8,128)(2,1)} %get-tuple-element.33), channel_id=1, source_target_pairs={{0,16},{8,24},{16,0},{24,8},{1,17},{9,25},{17,1},{25,9},{2,18},{10... | collective-permute-start | bytes 884744 | tf_op jit(solution)/shard_map/ppermute | solution.py:413
  16.0 16.2 %collective-permute-start.2 = (bf16[9,2,16,512]{3,2,1,0:T(8,128)(2,1)}, bf16[9,2,16,512]{3,2,1,0:T(8,128)(2,1)S(1)}, u32[]{:S(2)}, u32[]{:S(2)}) collective-permute-start(bf16[9,2,16,512]{3,2,1,0:T(8,128)(2,1)} %get-tuple-element.34), channel_id=1, source_target_pairs={{0,24},{8,16},{16,8},{24,0},{1,25},{9,17},{17,9},{25,1},{2,26},{10... | collective-permute-start | bytes 884744 | tf_op jit(solution)/shard_map/ppermute | solution.py:413
  16.9 15.3 %copy-start = (bf16[9,2,16,512]{3,2,1,0:T(8,128)(2,1)S(1)}, bf16[9,2,16,512]{3,2,1,0:T(8,128)(2,1)}, u32[]{:S(2)}) copy-start(bf16[9,2,16,512]{3,2,1,0:T(8,128)(2,1)} %get-tuple-element.31.pieces_0_) | copy-start | bytes 884740
where the time goes:
time: 33.3 us; the launch traced here: 33.1 us
  blocking collectives  12.9 us (39%)
  starting transfers between devices  10.9 us (33%)
  Pallas kernels  8.63 us (26%)
  between operations  0.72 us (2%)
    all_to_all x1, blocking collectives, local(): lax.all_to_all(grads, ('beam', 'ma'), split_axis=0, concat_axis=0, tiled=...  12.9 us
    all_to_all x1, starting transfers between devices, local(): lax.all_to_all(sent, ('beam', 'ma'), split_axis=0, concat_axis=0, tiled=T...  7.3 us
    ppermute x3, starting transfers between devices, exchange(): lax.ppermute(pieces[j], axis, [(i, i ^ j) for i in range(count)])  3.55 us
    pallas_call x1, Pallas kernels, local(): pl.pallas_call(functools.partial(tables_kernel, blocks_local, sky_devices...  3.07 us
    pallas_call x1, Pallas kernels, local(): pl.pallas_call(functools.partial(samples_kernel, blocks_local, rows), out...  2.39 us
    pallas_call x1, Pallas kernels, local(): pl.pallas_call(modes_kernel, out_shape=[jax.ShapeDtypeStruct((beams * sky...  2.29 us
    pallas_call x1, Pallas kernels, local(): pl.pallas_call(gradient_kernel, out_shape=jax.ShapeDtypeStruct((sky_order...  0.87 us
  transfers between devices with their start and end apart: 4, of which 0 were waited for; matrix products, arithmetic and copies ran while one was open for 0% of the time, Pallas kernels for 16%

commit v1 on v0

--- a/solution.py
+++ b/solution.py
@@ -77,9 +77,9 @@
 
 def modes_kernel(sky_hbm, beam_hbm, wigner_hbm, later_hbm, out, later, sky, beam, wigner, arrivals):
     chunks, orders, sky_orders, cycles, width = wigner.shape
-    small = bring((sky_hbm, beam_hbm), (sky, beam), arrivals, 0)
     spans = [pl.ds(i * width, width) for i in range(chunks)]
     large = bring([wigner_hbm.at[:, :, :, span] for span in spans], [wigner.at[i] for i in range(chunks)], arrivals, 2)
+    small = bring((sky_hbm, beam_hbm), (sky, beam), arrivals, 0)
     places = [
         place if place.shape == source.shape else place.at[0 : source.shape[0]]
         for source, place in zip(later_hbm, later)

time: 33.3 us -> 33.5 us (level)
  no operation moved by 1% of the time
where the time goes in v1:
time: 33.5 us; the launch traced here: 33.3 us
  blocking collectives  12.9 us (39%)
  starting transfers between devices  10.9 us (33%)
  Pallas kernels  8.84 us (26%)
  between operations  0.72 us (2%)
    all_to_all x1, blocking collectives, local(): lax.all_to_all(grads, ('beam', 'ma'), split_axis=0, concat_axis=0, tiled=...  12.9 us
    all_to_all x1, starting transfers between devices, local(): lax.all_to_all(sent, ('beam', 'ma'), split_axis=0, concat_axis=0, tiled=T...  7.3 us
    ppermute x3, starting transfers between devices, exchange(): lax.ppermute(pieces[j], axis, [(i, i ^ j) for i in range(count)])  3.55 us
    pallas_call x1, Pallas kernels, local(): pl.pallas_call(functools.partial(tables_kernel, blocks_local, sky_devices...  3.07 us
    pallas_call x1, Pallas kernels, local(): pl.pallas_call(modes_kernel, out_shape=[jax.ShapeDtypeStruct((beams * sky...  2.51 us
    pallas_call x1, Pallas kernels, local(): pl.pallas_call(functools.partial(samples_kernel, blocks_local, rows), out...  2.39 us
    pallas_call x1, Pallas kernels, local(): pl.pallas_call(gradient_kernel, out_shape=jax.ShapeDtypeStruct((sky_order...  0.87 us
  transfers between devices with their start and end apart: 4, of which 0 were waited for; matrix products, arithmetic and copies ran while one was open for 0% of the time, Pallas kernels for 16%

profile of v1, /device:TPU:0, one launch (start us, length us, event | category | flops | bytes accessed | tf_op | source)
XLA Modules:
  0.0 33.3 jit_solution(13828606631407952921)
XLA Ops:
  0.0 2.5 %modes.1 = (bf16[16,8,128]{2,1,0:T(8,128)(2,1)}, s32[16]{0:T(128)S(1)}, s32[128]{0:T(128)S(1)}, s32[128]{0:T(128)S(1)}, f32[128,128]{1,0:T(8,128)S(1)}, /*index=...) custom-call(f32[2,2,2048]{2,1,0:T(2,128)} %sky_hbm.1, f32[8,2,2048]{2,1,0:T(2,128)} %beam_hbm.3, ...), custom_call_target="tpu_custom_call" | custom-call | tf_op jit(solution)/shard_map/modes/pallas_call | solution.py:458
  2.5 7.3 %all-to-all-start = ((bf16[32,4,128]{2,1,0:T(4,128)(2,1)}), bf16[32,4,128]{2,1,0:T(4,128)(2,1)S(1)}, u32[]{:S(2)}, u32[]{:S(2)}) async-start(bf16[32,4,128]{2,1,0:T(4,128)(2,1)} %bitcast.5), calls=%async_computation | async-start | bytes 65536 | tf_op jit(solution)/shard_map/all_to_all | solution.py:479
  9.8 3.1 %tables.1 = (bf16[4096,128]{1,0:T(8,128)(2,1)S(1)}, bf16[4096,128]{1,0:T(8,128)(2,1)S(1)}, bf16[1024,128]{1,0:T(8,128)(2,1)S(1)}, bf16[9,2,16,512]{3,2,1,0:T(8,1...) custom-call(s32[16]{0:T(128)S(1)} %get-tuple-element.24.order_vmem, ...), custom_call_target="tpu_custom_call" | custom-call | flops 100000000 | bytes 4000000 | tf_op jit(solution)/shard_map/tables/pallas_call | solution.py:483
  12.9 1.8 %collective-permute-start = (bf16[9,2,16,512]{3,2,1,0:T(8,128)(2,1)}, bf16[9,2,16,512]{3,2,1,0:T(8,128)(2,1)S(1)}, u32[]{:S(2)}, u32[]{:S(2)}) collective-permute-start(bf16[9,2,16,512]{3,2,1,0:T(8,128)(2,1)} %get-tuple-element.32), channel_id=1, source_target_pairs={{0,8},{8,0},{16,24},{24,16},{1,9},{9,1},{17,25},{25,17},{2,10},{10... | collective-permute-start | bytes 884744 | tf_op jit(solution)/shard_map/ppermute | solution.py:413
  14.7 1.5 %collective-permute-start.1 = (bf16[9,2,16,512]{3,2,1,0:T(8,128)(2,1)}, bf16[9,2,16,512]{3,2,1,0:T(8,128)(2,1)S(1)}, u32[]{:S(2)}, u32[]{:S(2)}) collective-permute-start(bf16[9,2,16,512]{3,2,1,0:T(8,128)(2,1)} %get-tuple-element.33), channel_id=1, source_target_pairs={{0,16},{8,24},{16,0},{24,8},{1,17},{9,25},{17,1},{25,9},{2,18},{10... | collective-permute-start | bytes 884744 | tf_op jit(solution)/shard_map/ppermute | solution.py:413
  16.2 0.3 collective-permute-start.2
  17.1 0.0 all-to-all-done
  17.1 0.0 copy-start
  17.1 2.4 %samples.1 = bf16[4,32,128]{2,1,0:T(8,128)(2,1)S(1)} custom-call(s32[128]{0:T(128)S(1)} %get-tuple-element.20.owners_vmem, s32[128]{0:T(128)S(1)} %get-tuple-element.21.locals_vmem, s32[8,128]{1,0:T(8,128)S(1)} %broadcast_in_dim.9.count, f32[128,128]{1,0:T(8,128)S(1)} %get-tuple-element.22.noise, bf16[128,128]{1,0:T(8,128)(2,1)S(1)} %bitcast.11, ...), custom_call_target="tpu_custom_call" | custom-call | flops 40000000000 | bytes 100000000 | tf_op jit(solution)/shard_map/samples/pallas_call | solution.py:513
  19.5 12.9 %all_to_all.10 = bf16[32,4,128]{2,1,0:T(4,128)(2,1)S(1)} all-to-all(bf16[32,4,128]{2,1,0:T(4,128)(2,1)S(1)} %bitcast.12), channel_id=1, replica_groups=mesh['beam'=4,'ma'=8] {'beam','ma'}, dimensions={0} | all-to-all | bytes 65536 | tf_op jit(solution)/shard_map/all_to_all | solution.py:539
  32.4 0.0 collective-permute-done.pieces_1_
  32.4 0.0 collective-permute-done.1.pieces_2_
  32.4 0.0 collective-permute-done.2.pieces_3_
  32.4 0.0 copy-done
  32.4 0.9 %gradient.1 = f32[2,2,512]{2,1,0:T(2,128)} custom-call(bf16[4,32,128]{2,1,0:T(8,128)(2,1)S(1)} %bitcast.10, bf16[9,2,16,512]{3,2,1,0:T(8,128)(2,1)S(1)} %copy-done, bf16[9,2,16,512]{3,2,1,0:T(8,128)(2,1)S(1)} %collective-permute-done.pieces_1_, bf16[9,2,16,512]{3,2,1,0:T(8,128)(2,1)S(1)} %collective-permute-done.1.pieces_2_, ...), custom_call_target="tpu_custom_call" | custom-call | tf_op jit(solution)/shard_map/gradient/pallas_call | solution.py:540
  (1 shorter events, 0.0 us)
Async XLA Ops:
  2.5 14.6 %all-to-all-start = ((bf16[32,4,128]{2,1,0:T(4,128)(2,1)}), bf16[32,4,128]{2,1,0:T(4,128)(2,1)S(1)}, u32[]{:S(2)}, u32[]{:S(2)}) async-start(bf16[32,4,128]{2,1,0:T(4,128)(2,1)} %bitcast.5), calls=%async_computation | async-start | bytes 65536 | tf_op jit(solution)/shard_map/all_to_all | solution.py:479
  12.9 19.5 %collective-permute-start = (bf16[9,2,16,512]{3,2,1,0:T(8,128)(2,1)}, bf16[9,2,16,512]{3,2,1,0:T(8,128)(2,1)S(1)}, u32[]{:S(2)}, u32[]{:S(2)}) collective-permute-start(bf16[9,2,16,512]{3,2,1,0:T(8,128)(2,1)} %get-tuple-element.32), channel_id=1, source_target_pairs={{0,8},{8,0},{16,24},{24,16},{1,9},{9,1},{17,25},{25,17},{2,10},{10... | collective-permute-start | bytes 884744 | tf_op jit(solution)/shard_map/ppermute | solution.py:413
  14.7 17.7 %collective-permute-start.1 = (bf16[9,2,16,512]{3,2,1,0:T(8,128)(2,1)}, bf16[9,2,16,512]{3,2,1,0:T(8,128)(2,1)S(1)}, u32[]{:S(2)}, u32[]{:S(2)}) collective-permute-start(bf16[9,2,16,512]{3,2,1,0:T(8,128)(2,1)} %get-tuple-element.33), channel_id=1, source_target_pairs={{0,16},{8,24},{16,0},{24,8},{1,17},{9,25},{17,1},{25,9},{2,18},{10... | collective-permute-start | bytes 884744 | tf_op jit(solution)/shard_map/ppermute | solution.py:413
  16.2 16.2 %collective-permute-start.2 = (bf16[9,2,16,512]{3,2,1,0:T(8,128)(2,1)}, bf16[9,2,16,512]{3,2,1,0:T(8,128)(2,1)S(1)}, u32[]{:S(2)}, u32[]{:S(2)}) collective-permute-start(bf16[9,2,16,512]{3,2,1,0:T(8,128)(2,1)} %get-tuple-element.34), channel_id=1, source_target_pairs={{0,24},{8,16},{16,8},{24,0},{1,25},{9,17},{17,9},{25,1},{2,26},{10... | collective-permute-start | bytes 884744 | tf_op jit(solution)/shard_map/ppermute | solution.py:413
  17.1 15.3 %copy-start = (bf16[9,2,16,512]{3,2,1,0:T(8,128)(2,1)S(1)}, bf16[9,2,16,512]{3,2,1,0:T(8,128)(2,1)}, u32[]{:S(2)}) copy-start(bf16[9,2,16,512]{3,2,1,0:T(8,128)(2,1)} %get-tuple-element.31.pieces_0_) | copy-start | bytes 884740
